TPU v7x, 512 devices: a whole 4x8x8 slice. The times are simulated.
512 devices in a mesh: ctx: 64 (over x, z, core), tp: 8 (over y).
Axes of the slice: x: 4, y: 8, z: 8, core: 2. Of those that a mesh axis runs over, the one named last changes fastest.
Arguments:
- features: bfloat16 [128, 196, 1152], P('ctx', None, 'tp'), may hold values from -6 to 6
- group_kernel: bfloat16 [9, 1152, 48], P(None, 'tp'), may hold values from -0.3125 to 0.3125
- squeeze_in: bfloat16 [1152, 288], P('tp'), may hold values from -0.75 to 0.75
- squeeze_out: bfloat16 [288, 1152], P(None, 'tp'), may hold values from -0.75 to 0.75
- sampler_kernel: bfloat16 [1152, 8, 1152], P('ctx', None, 'tp'), may hold values from -0.0625 to 0.0625
- readout_kernel: bfloat16 [1152, 8192], P('ctx', 'tp'), may hold values from -0.1875 to 0.1875
- frame_clip: int32 [128], replicated, may hold values from 0 to 15, as said below
- clip_keep: int32 [16], replicated, may hold values from 1 to 512, as said below
- token_cotangent: bfloat16 [4096, 8192], P('ctx', 'tp'), may hold values from -6 to 6
Outputs:
- llm_tokens: bfloat16 [4096, 8192], P('ctx', 'tp')
- grad_features: bfloat16 [128, 196, 1152], P('ctx', None, 'tp')
Inputs may be any that keep to these rules, and one draw needn't show every extreme that they name: `frame_clip`: clip ids start at 0 and never fall along the frames; every clip covers an even number of frames from 2 to 16 and starts at an even frame; some clip covers 16. `clip_keep`: each clip keeps at least one and at most 8 * 8 times half its frames of its tokens; the clip of 16 frames keeps all of its tokens, and some clip keeps a single token.
All inputs are finite; a program needn't handle non-finite values.
Results may differ from a plain program's by a relative error of at most 0.009.
Values may be sent and summed in bfloat16 or wider, within the bound.
A program may use at most 64 MiB of HBM per device.

v0:
```python
import jax
import jax.numpy as jnp
from jax import lax
from jax.sharding import PartitionSpec as P

SIDE = 14
OUT_SIDE = 8


def shifted(value, axis, by):
    count = lax.axis_size(axis)
    pairs = [(i, i + by) for i in range(count) if 0 <= i + by < count]
    return lax.ppermute(value, axis, pairs)


def silu_slope(values):
    sigma = jax.nn.sigmoid(values)
    return sigma * (1.0 + values * (1.0 - sigma))


def grouped_forward(frames_grid, group_kernel):
    count, side, _, chans = frames_grid.shape
    width = group_kernel.shape[2]
    groups = chans // width
    padded = jnp.pad(frames_grid, ((0, 0), (1, 1), (1, 1), (0, 0)))
    kernel = group_kernel.reshape(9, groups, width, width)
    total = jnp.zeros((count, side, side, groups, width), jnp.float32)
    for kernel_tap in range(9):
        row_shift, col_shift = divmod(kernel_tap, 3)
        window = padded[:, row_shift : row_shift + side, col_shift : col_shift + side]
        window = window.reshape(count, side, side, groups, width)
        total = total + jnp.einsum(
            "fyxgi,gio->fyxgo", window, kernel[kernel_tap], preferred_element_type=jnp.float32
        )
    return total.reshape(count, side, side, chans)


def grouped_backward(grad_grid, group_kernel):
    count, side, _, chans = grad_grid.shape
    width = group_kernel.shape[2]
    groups = chans // width
    kernel = group_kernel.reshape(9, groups, width, width)
    source = grad_grid.reshape(count, side, side, groups, width)
    total = jnp.zeros((count, side + 2, side + 2, chans), jnp.float32)
    for kernel_tap in range(9):
        row_shift, col_shift = divmod(kernel_tap, 3)
        spread = jnp.einsum(
            "fyxgo,gio->fyxgi", source, kernel[kernel_tap], preferred_element_type=jnp.float32
        )
        spread = spread.reshape(count, side, side, chans)
        total = total + jnp.pad(
            spread, ((0, 0), (row_shift, 2 - row_shift), (col_shift, 2 - col_shift), (0, 0))
        )
    return total[:, 1 : side + 1, 1 : side + 1]


def make_patches(prev_odd, even):
    stacked = jnp.stack([prev_odd, even], axis=1)
    stacked = jnp.pad(stacked, ((0, 0), (0, 0), (1, 1), (1, 1), (0, 0)))
    pairs, _, padded_side, _, chans = stacked.shape
    half = padded_side // 2
    shaped = stacked.reshape(pairs, 2, half, 2, half, 2, chans).transpose(0, 2, 4, 1, 3, 5, 6)
    return shaped.reshape(pairs * half * half, 8 * chans)


def unpatch(grad_rows, pairs, side, chans):
    half = side // 2 + 1
    shaped = grad_rows.reshape(pairs, half, half, 2, 2, 2, chans).transpose(0, 3, 1, 4, 2, 5, 6)
    shaped = shaped.reshape(pairs, 2, 2 * half, 2 * half, chans)
    return shaped[:, :, 1 : side + 1, 1 : side + 1]


def contract_last(left, right):
    return lax.dot_general(
        left, right, (((1,), (1,)), ((), ())), preferred_element_type=jnp.float32
    )


def per_device(
    features,
    group_kernel,
    squeeze_in,
    squeeze_out,
    sampler_kernel,
    readout_kernel,
    frame_clip,
    clip_keep,
    token_cotangent,
):
    highest = lax.Precision.HIGHEST
    shard_index = lax.axis_index("ctx")
    frames_dev, cells, chans = features.shape
    pairs_dev = frames_dev // 2
    grid = features.reshape(frames_dev, SIDE, SIDE, chans)
    conv_out = grouped_forward(grid, group_kernel)
    active = jax.nn.silu(conv_out)
    pooled = jnp.mean(active, axis=(1, 2))
    squeezed = lax.psum(jnp.dot(pooled, squeeze_in.astype(jnp.float32), precision=highest), "tp")
    relaxed = jax.nn.silu(squeezed)
    excite = jax.nn.sigmoid(jnp.dot(relaxed, squeeze_out.astype(jnp.float32), precision=highest))
    hidden = (grid.astype(jnp.float32) + active * excite[:, None, None, :]).astype(jnp.bfloat16)
    full_sampler, full_readout = (
        lax.all_gather(sampler_kernel, "ctx", axis=0, tiled=True),
        lax.all_gather(readout_kernel, "ctx", axis=0, tiled=True),
    )
    sampler_rows = full_sampler.reshape(full_sampler.shape[0], 8 * chans)
    halo_frame = shifted(hidden[-1], "ctx", 1)
    local_clip = lax.dynamic_slice_in_dim(frame_clip, shard_index * frames_dev, frames_dev)
    edge_clip = lax.dynamic_slice_in_dim(
        frame_clip, jnp.maximum(shard_index * frames_dev - 1, 0), 1
    )
    first_keep = jnp.logical_and(shard_index > 0, edge_clip[0] == local_clip[0])
    later_keep = local_clip[1:-1:2] == local_clip[2::2]
    pair_mask = jnp.concatenate([first_keep[None], later_keep]).astype(jnp.float32)
    even = hidden[0::2]
    odd = hidden[1::2]
    prev_odd = jnp.concatenate([halo_frame[None], odd[:-1]], axis=0)
    prev_odd = prev_odd * pair_mask.astype(jnp.bfloat16)[:, None, None, None]
    patches = make_patches(prev_odd, even)
    per_frame = OUT_SIDE * OUT_SIDE
    pair_clip = frame_clip[0::2]
    clip_ids = jnp.arange(clip_keep.shape[0], dtype=jnp.int32)
    start_pair = jnp.sum((pair_clip[None, :] < clip_ids[:, None]).astype(jnp.int32), axis=1)
    own_clip = local_clip[0::2]
    one_hot = (own_clip[:, None] == clip_ids[None, :]).astype(jnp.int32)
    own_start = jnp.sum(one_hot * start_pair[None, :], axis=1)
    own_keep = jnp.sum(one_hot * clip_keep[None, :], axis=1)
    pair_index = shard_index * pairs_dev + jnp.arange(pairs_dev, dtype=jnp.int32)
    position = (pair_index - own_start)[:, None] * per_frame + jnp.arange(
        per_frame, dtype=jnp.int32
    )[None, :]
    live = (position < own_keep[:, None]).reshape(-1).astype(jnp.bfloat16)
    pre = lax.psum(contract_last(patches, sampler_rows), "tp")
    act = jax.nn.silu(pre).astype(jnp.bfloat16)
    tokens = (
        jnp.dot(act, full_readout, preferred_element_type=jnp.float32).astype(jnp.bfloat16)
        * live[:, None]
    )
    llm_tokens = lax.all_to_all(tokens, "ctx", split_axis=0, concat_axis=0, tiled=True)
    back = (
        lax.all_to_all(token_cotangent, "ctx", split_axis=0, concat_axis=0, tiled=True)
        * live[:, None]
    )
    grad_act = lax.psum(contract_last(back, full_readout), "tp")
    grad_pre = (grad_act * silu_slope(pre)).astype(jnp.bfloat16)
    grad_patches = jnp.dot(grad_pre, sampler_rows, preferred_element_type=jnp.float32)
    grad_taps = unpatch(grad_patches, pairs_dev, SIDE, chans)
    leading = grad_taps[:, 0] * pair_mask[:, None, None, None]
    incoming = shifted(leading[0].astype(jnp.bfloat16), "ctx", -1).astype(jnp.float32)
    grad_even = grad_taps[:, 1]
    grad_odd = jnp.concatenate([leading[1:], incoming[None]], axis=0)
    grad_hidden = jnp.stack([grad_even, grad_odd], axis=1).reshape(frames_dev, SIDE, SIDE, chans)
    grad_excite = jnp.sum(grad_hidden * active, axis=(1, 2))
    grad_inner = grad_excite * excite * (1.0 - excite)
    grad_relaxed = lax.psum(
        jnp.dot(grad_inner, squeeze_out.astype(jnp.float32).T, precision=highest), "tp"
    )
    grad_squeezed = grad_relaxed * silu_slope(squeezed)
    grad_pooled = jnp.dot(grad_squeezed, squeeze_in.astype(jnp.float32).T, precision=highest)
    grad_active = grad_hidden * excite[:, None, None, :] + grad_pooled[:, None, None, :] / cells
    grad_conv = (grad_active * silu_slope(conv_out)).astype(jnp.bfloat16)
    grad_grid = grad_hidden + grouped_backward(grad_conv, group_kernel)
    grad_features = grad_grid.astype(jnp.bfloat16).reshape(frames_dev, cells, chans)
    return (llm_tokens, grad_features)


def solution(mesh):
    placed = (
        P("ctx", None, "tp"),
        P(None, "tp", None),
        P("tp", None),
        P(None, "tp"),
        P("ctx", None, "tp"),
        P("ctx", "tp"),
        P(),
        P(),
        P("ctx", "tp"),
    )
    return jax.shard_map(
        per_device,
        mesh=mesh,
        in_specs=placed,
        out_specs=(P("ctx", "tp"), P("ctx", None, "tp")),
        check_vma=False,
    )
```

profile of v0, /device:TPU:6, one launch (start us, length us, event | category | flops | bytes accessed | tf_op | source)
XLA Modules:
  0.0 348.0 jit_solution(8308310035529797624)
XLA Ops:
  8.7 1.1 copy.230
  9.7 1.0 copy.240
  10.8 1.5 fusion.52
  12.4 2.3 pad_slice_fusion
  17.0 1.2 reshape.191
  18.2 0.8 copy.246
  19.0 2.0 reshape.192
  21.2 2.0 reshape.193
  27.1 17.6 %psum.28 = f32[2,288]{1,0:T(2,128)S(1)} all-reduce(f32[2,288]{1,0:T(2,128)S(1)} %fusion.54), channel_id=1, replica_groups=mesh['ctx'=64,'tp'=8] {'tp'}, use_global_device_ids=true, to_apply=%region_1.2 | all-reduce | flops 576 | bytes 4608 | tf_op jit(solution)/shard_map/psum | solution.py:98
  45.6 1.4 add_convert_fusion
  47.2 1.9 collective-permute-start
  51.1 15.2 %all-to-all-start.1 = ((bf16[64,2,512]{2,1,0:T(2,128)(2,1)}), bf16[64,2,512]{2,1,0:T(2,128)(2,1)S(1)}, u32[]{:S(2)}, u32[]{:S(2)}) async-start(bf16[64,2,512]{2,1,0:T(2,128)(2,1)} %reshape.225), calls=%async_computation.1 | async-start | bytes 262144 | tf_op jit(solution)/shard_map/all_to_all | solution.py:141
  71.6 0.9 reshape.196
  72.5 2.6 all-to-all-done.1
  75.3 24.2 %all-gather.6.cloned.1.call-done = bf16[64,18,1024]{2,1,0:T(8,128)(2,1)} async-done(((bf16[1,18,1024]{2,1,0:T(8,128)(2,1)}), bf16[64,18,1024]{2,1,0:T(8,128)(2,1)}) %all-gather.6.cloned.1.call-update) | async-done | bytes 2359312 | tf_op jit(solution)/shard_map/all_gather | solution.py:104
  99.5 2.9 reshape.212
  102.4 1.6 fusion.29
  104.0 81.3 %all-gather.4.cloned.1.call-done = bf16[1152,8,144]{2,1,0:T(8,128)(2,1)} async-done(((bf16[18,8,144]{2,1,0:T(8,128)(2,1)}), bf16[1152,8,144]{2,1,0:T(8,128)(2,1)}) %all-gather.4.cloned.1.call-update) | async-done | bytes 2654224 | tf_op jit(solution)/shard_map/all_gather | solution.py:103
  185.3 5.5 %copy.254 = bf16[1152,8,144]{0,2,1:T(8,128)(2,1)S(1)} copy(bf16[1152,8,144]{2,1,0:T(8,128)(2,1)} %all-gather.4.cloned.1.call-done) | data formatting | bytes 5308416 | tf_op jit(solution)/shard_map/all_gather | solution.py:103
  190.8 2.2 fusion.55
  193.1 77.1 %all-reduce.14.cloned.1.call-done = (f32[64,1152]{1,0:T(8,128)}, f32[64,1152]{1,0:T(8,128)}) async-done(((f32[64,1152]{1,0:T(8,128)}, f32[64,1152]{1,0:T(8,128)}), (f32[64,1152]{1,0:T(8,128)}, f32[64,1152]{1,0:T(8,128)})) %all-reduce.14.cloned.1.call-update) | async-done | bytes 589840 | tf_op jit(solution)/shard_map/psum | solution.py:144
  270.3 2.3 convolution_bitcast_fusion.14
  273.0 0.8 fusion.51
  273.8 2.1 collective-permute-start.1
  278.1 11.2 %all-to-all-start = ((bf16[64,2,512]{2,1,0:T(2,128)(2,1)}), bf16[64,2,512]{2,1,0:T(2,128)(2,1)S(1)}, u32[]{:S(2)}, u32[]{:S(2)}) async-start(bf16[64,2,512]{2,1,0:T(2,128)(2,1)} %reshape.227), calls=%async_computation | async-start | bytes 262144 | tf_op jit(solution)/shard_map/all_to_all | solution.py:139
  290.1 16.7 %psum.31 = f32[2,288]{1,0:T(2,128)S(1)} all-reduce(f32[2,288]{1,0:T(2,128)S(1)} %fusion.39), channel_id=1, replica_groups=mesh['ctx'=64,'tp'=8] {'tp'}, use_global_device_ids=true, to_apply=%region_8.9 | all-reduce | flops 576 | bytes 4608 | tf_op jit(solution)/shard_map/psum | solution.py:155
  308.1 1.1 convolution_bitcast_fusion.7
  309.2 1.1 convolution_bitcast_fusion.6
  310.3 1.1 convolution_bitcast_fusion.5
  311.4 1.1 convolution_bitcast_fusion.4
  312.6 1.1 convolution_bitcast_fusion.3
  314.8 1.3 reshape.201
  316.2 1.5 copy.264
  317.7 1.4 reshape.202
  319.0 1.5 copy.265
  320.5 1.4 reshape.203
  321.9 1.5 copy.266
  323.4 1.4 reshape.204
  324.8 1.5 copy.267
  326.3 1.4 reshape.205
  327.7 1.5 copy.268
  329.2 1.3 reshape.206
  330.9 1.4 reshape.207
  332.7 1.4 reshape.208
  334.5 1.4 reshape.209
  335.9 1.5 pad_add_fusion
  337.4 2.4 fusion.15
  339.8 0.8 copy.272
  (156 shorter events, 22.5 us)
Async XLA Ops:
  7.2 38.1 %copy-start = (bf16[288,144]{0,1:T(8,128)(2,1)S(1)}, bf16[288,144]{0,1:T(8,128)(2,1)}, u32[]{:S(2)}) copy-start(bf16[288,144]{0,1:T(8,128)(2,1)} %param.12) | copy-start | bytes 248836
  7.2 92.3 %all-gather.6.cloned.1.call-start = ((), (), s32[]{:S(2)}) async-start(), calls=%async_computation.3 | async-start | bytes 3194880 | tf_op jit(solution)/shard_map/all_gather | solution.py:104
  7.9 177.4 %all-gather.4.cloned.1.call-start = ((), (), s32[]{:S(2)}) async-start(), calls=%async_computation.2 | async-start | bytes 4792320 | tf_op jit(solution)/shard_map/all_gather | solution.py:103
  15.1 8.3 %copy-start.9 = (bf16[1,144,48]{2,1,0:T(8,128)(2,1)}, bf16[1,144,48]{2,1,0:T(8,128)(2,1)S(1)}, u32[]{:S(2)}) copy-start(bf16[1,144,48]{2,1,0:T(8,128)(2,1)S(1)} %copy.233) | copy-start | bytes 41476
  15.5 8.2 %copy-start.11 = (bf16[1,144,48]{2,1,0:T(8,128)(2,1)}, bf16[1,144,48]{2,1,0:T(8,128)(2,1)S(1)}, u32[]{:S(2)}) copy-start(bf16[1,144,48]{2,1,0:T(8,128)(2,1)S(1)} %copy.235) | copy-start | bytes 41476
  15.8 8.0 %copy-start.13 = (bf16[1,144,48]{2,1,0:T(8,128)(2,1)}, bf16[1,144,48]{2,1,0:T(8,128)(2,1)S(1)}, u32[]{:S(2)}) copy-start(bf16[1,144,48]{2,1,0:T(8,128)(2,1)S(1)} %copy.237) | copy-start | bytes 41476
  16.2 7.9 %copy-start.15 = (bf16[1,144,48]{2,1,0:T(8,128)(2,1)}, bf16[1,144,48]{2,1,0:T(8,128)(2,1)S(1)}, u32[]{:S(2)}) copy-start(bf16[1,144,48]{2,1,0:T(8,128)(2,1)S(1)} %copy.239) | copy-start | bytes 41476
  16.6 7.8 %copy-start.17 = (bf16[1,144,48]{2,1,0:T(8,128)(2,1)}, bf16[1,144,48]{2,1,0:T(8,128)(2,1)S(1)}, u32[]{:S(2)}) copy-start(bf16[1,144,48]{2,1,0:T(8,128)(2,1)S(1)} %copy.242) | copy-start | bytes 41476
  16.9 7.7 %copy-start.19 = (bf16[1,144,48]{2,1,0:T(8,128)(2,1)}, bf16[1,144,48]{2,1,0:T(8,128)(2,1)S(1)}, u32[]{:S(2)}) copy-start(bf16[1,144,48]{2,1,0:T(8,128)(2,1)S(1)} %copy.244) | copy-start | bytes 41476
  19.0 5.9 %copy-start.21 = (bf16[1,144,48]{2,1,0:T(8,128)(2,1)}, bf16[1,144,48]{2,1,0:T(8,128)(2,1)S(1)}, u32[]{:S(2)}) copy-start(bf16[1,144,48]{2,1,0:T(8,128)(2,1)S(1)} %copy.246) | copy-start | bytes 41476
  21.2 4.2 %copy-start.23 = (bf16[1,144,48]{2,1,0:T(8,128)(2,1)}, bf16[1,144,48]{2,1,0:T(8,128)(2,1)S(1)}, u32[]{:S(2)}) copy-start(bf16[1,144,48]{2,1,0:T(8,128)(2,1)S(1)} %copy.248) | copy-start | bytes 41476
  24.1 1.0 copy-start.7
  24.4 1.0 copy-start.8
  25.4 1.5 copy-start.26
  25.8 23.9 %copy-start.25 = (bf16[64,1024]{1,0:T(8,128)(2,1)S(1)}, bf16[64,1024]{1,0:T(8,128)(2,1)}, u32[]{:S(2)}) copy-start(bf16[64,1024]{1,0:T(8,128)(2,1)} %param.17) | copy-start | bytes 393220
  26.3 40.2 %copy-start.33 = (s32[128]{0:T(128)S(1)}, s32[128]{0:T(128)}, u32[]{:S(2)}) copy-start(s32[128]{0:T(128)} %param.15) | copy-start | bytes 1540
  26.3 43.2 %copy-start.34 = (s32[16]{0:T(128)S(1)}, s32[16]{0:T(128)}, u32[]{:S(2)}) copy-start(s32[16]{0:T(128)} %param.16) | copy-start | bytes 196
  44.7 0.6 copy-start.28
  47.2 23.6 %collective-permute-start = (bf16[14,14,144]{2,1,0:T(8,128)(2,1)S(1)}, bf16[14,14,144]{2,1,0:T(8,128)(2,1)S(1)}, u32[]{:S(2)}, u32[]{:S(2)}) collective-permute-start(bf16[14,14,144]{2,1,0:T(8,128)(2,1)S(1)} %bitcast.239), channel_id=1, source_target_pairs={{0,8},{8,16},{16,24},{24,32},{32,40},{40,48},{48,56},{56,64},{64,7... | collective-permute-start | bytes 169352 | tf_op jit(solution)/shard_map/ppermute | solution.py:13
  51.1 24.1 %all-to-all-start.1 = ((bf16[64,2,512]{2,1,0:T(2,128)(2,1)}), bf16[64,2,512]{2,1,0:T(2,128)(2,1)S(1)}, u32[]{:S(2)}, u32[]{:S(2)}) async-start(bf16[64,2,512]{2,1,0:T(2,128)(2,1)} %reshape.225), calls=%async_computation.1 | async-start | bytes 262144 | tf_op jit(solution)/shard_map/all_to_all | solution.py:141
  66.3 204.0 %all-reduce.14.cloned.1.call-start = ((), (), s32[]{:S(2)}) async-start(), calls=%async_computation.4 | async-start | bytes 1179648 | tf_op jit(solution)/shard_map/psum | solution.py:144
  70.8 31.6 %copy-start.30 = (bf16[64]{0:T(256)(128)(2,1)}, bf16[64]{0:T(256)(128)(2,1)S(1)}, u32[]{:S(2)}) copy-start(bf16[64]{0:T(256)(128)(2,1)S(1)} %compare_convert_fusion) | copy-start | bytes 388
  102.4 1.6 copy-start.1
  270.3 5.6 %copy-start.2 = (bf16[1152,1024]{1,0:T(8,128)(2,1)S(1)}, bf16[1152,1024]{1,0:T(8,128)(2,1)}, u32[]{:S(2)}) copy-start(bf16[1152,1024]{1,0:T(8,128)(2,1)} %copy-done.1) | copy-start | bytes 7077892
  270.3 5.6 %copy-start.31 = (bf16[64]{0:T(256)(128)(2,1)S(1)}, bf16[64]{0:T(256)(128)(2,1)}, u32[]{:S(2)}) copy-start(bf16[64]{0:T(256)(128)(2,1)} %copy-done.30) | copy-start | bytes 388
  270.3 5.6 %copy-start.32 = (f32[64,1152]{1,0:T(8,128)S(1)}, f32[64,1152]{1,0:T(8,128)}, u32[]{:S(2)}) copy-start(f32[64,1152]{1,0:T(8,128)} %get-tuple-element.15) | copy-start | bytes 884740
  273.8 15.7 %copy-start.3 = (f32[2,14,14,144]{3,0,2,1:T(2,128)S(1)}, f32[2,14,14,144]{3,0,2,1:T(2,128)}, u32[]{:S(2)}) copy-start(f32[2,14,14,144]{3,0,2,1:T(2,128)} %get-tuple-element.17) | copy-start | bytes 677380
  273.8 33.1 %copy-start.27 = (bf16[144,288]{1,0:T(8,128)(2,1)S(1)}, bf16[144,288]{1,0:T(8,128)(2,1)}, u32[]{:S(2)}) copy-start(bf16[144,288]{1,0:T(8,128)(2,1)} %param.11) | copy-start | bytes 248836
  273.8 33.1 %copy-start.29 = (f32[2,288]{1,0:T(2,128)S(1)}, f32[2,288]{1,0:T(2,128)}, u32[]{:S(2)}) copy-start(f32[2,288]{1,0:T(2,128)} %copy-done.28) | copy-start | bytes 6916
  273.8 15.5 %collective-permute-start.1 = (bf16[14,14,144]{2,1,0:T(8,128)(2,1)S(1)}, bf16[14,14,144]{2,1,0:T(8,128)(2,1)S(1)}, u32[]{:S(2)}, u32[]{:S(2)}) collective-permute-start(bf16[14,14,144]{2,1,0:T(8,128)(2,1)S(1)} %fusion.31), channel_id=1, source_target_pairs={{8,0},{16,8},{24,16},{32,24},{40,32},{48,40},{56,48},{64,56},{72,6... | collective-permute-start | bytes 169352 | tf_op jit(solution)/shard_map/ppermute | solution.py:13
  278.1 62.5 %all-to-all-start = ((bf16[64,2,512]{2,1,0:T(2,128)(2,1)}), bf16[64,2,512]{2,1,0:T(2,128)(2,1)S(1)}, u32[]{:S(2)}, u32[]{:S(2)}) async-start(bf16[64,2,512]{2,1,0:T(2,128)(2,1)} %reshape.227), calls=%async_computation | async-start | bytes 262144 | tf_op jit(solution)/shard_map/all_to_all | solution.py:139
  289.3 18.8 %copy-start.10 = (bf16[1,144,48]{2,1,0:T(8,128)(2,1)S(1)}, bf16[1,144,48]{2,1,0:T(8,128)(2,1)}, u32[]{:S(2)}) copy-start(bf16[1,144,48]{2,1,0:T(8,128)(2,1)} %copy-done.9) | copy-start | bytes 41476
  290.1 19.1 %copy-start.12 = (bf16[1,144,48]{2,1,0:T(8,128)(2,1)S(1)}, bf16[1,144,48]{2,1,0:T(8,128)(2,1)}, u32[]{:S(2)}) copy-start(bf16[1,144,48]{2,1,0:T(8,128)(2,1)} %copy-done.11) | copy-start | bytes 41476
  307.5 2.9 copy-start.14
  307.5 3.9 %copy-start.16 = (bf16[1,144,48]{2,1,0:T(8,128)(2,1)S(1)}, bf16[1,144,48]{2,1,0:T(8,128)(2,1)}, u32[]{:S(2)}) copy-start(bf16[1,144,48]{2,1,0:T(8,128)(2,1)} %copy-done.15) | copy-start | bytes 41476
  307.9 4.7 %copy-start.18 = (bf16[1,144,48]{2,1,0:T(8,128)(2,1)S(1)}, bf16[1,144,48]{2,1,0:T(8,128)(2,1)}, u32[]{:S(2)}) copy-start(bf16[1,144,48]{2,1,0:T(8,128)(2,1)} %copy-done.17) | copy-start | bytes 41476
  308.1 5.5 %copy-start.20 = (bf16[1,144,48]{2,1,0:T(8,128)(2,1)S(1)}, bf16[1,144,48]{2,1,0:T(8,128)(2,1)}, u32[]{:S(2)}) copy-start(bf16[1,144,48]{2,1,0:T(8,128)(2,1)} %copy-done.19) | copy-start | bytes 41476
  309.2 4.7 %copy-start.22 = (bf16[1,144,48]{2,1,0:T(8,128)(2,1)S(1)}, bf16[1,144,48]{2,1,0:T(8,128)(2,1)}, u32[]{:S(2)}) copy-start(bf16[1,144,48]{2,1,0:T(8,128)(2,1)} %copy-done.21) | copy-start | bytes 41476
  310.3 3.8 %copy-start.24 = (bf16[1,144,48]{2,1,0:T(8,128)(2,1)S(1)}, bf16[1,144,48]{2,1,0:T(8,128)(2,1)}, u32[]{:S(2)}) copy-start(bf16[1,144,48]{2,1,0:T(8,128)(2,1)} %copy-done.23) | copy-start | bytes 41476
  332.3 3.6 %copy-start.4 = (f32[2,14,14,144]{3,0,2,1:T(2,128)S(1)}, f32[2,14,14,144]{3,0,2,1:T(2,128)}, u32[]{:S(2)}) copy-start(f32[2,14,14,144]{3,0,2,1:T(2,128)} %reshape.201) | copy-start | bytes 677380
  334.1 3.3 copy-start.5
  334.5 2.9 copy-start.6
Sparse Core Ops, SparseCore 0:
  11.3 88.0 all-gather.5
  102.8 82.4 all-gather.3
  193.2 77.0 all-reduce.13
where the time goes:
time: 349 us; the launch traced here: 348 us
  waiting for transfers between devices  187 us (54%)
  local copies, waits for them, and re-layouts  54.8 us (16%)
  blocking collectives  34.3 us (10%)
  starting transfers between devices  30.7 us (9%)
  matrix products  16 us (5%)
  between operations  15.9 us (5%)
  other arithmetic  9.59 us (3%)
    all_gather x1, waiting for transfers between devices, per_device(): lax.all_gather(sampler_kernel, 'ctx', axis=0, tiled=True)  81.3 us
    psum x1, waiting for transfers between devices, per_device(): grad_act = lax.psum(contract_last(back, full_readout), 'tp')  77.1 us
    all_gather x1, waiting for transfers between devices, per_device(): lax.all_gather(readout_kernel, 'ctx', axis=0, tiled=True)  24.2 us
    psum x1, blocking collectives, per_device(): lax.psum(jnp.dot(pooled, squeeze_in.astype(jnp.float32), precision=highes...  17.6 us
    psum x1, blocking collectives, per_device(): lax.psum(jnp.dot(grad_inner, squeeze_out.astype(jnp.float32).T, precision...  16.7 us
    all_to_all x1, starting transfers between devices, per_device(): lax.all_to_all(token_cotangent, 'ctx', split_axis=0, concat_axis=0, tiled...  15.2 us
    reshape x9, local copies, waits for them, and re-layouts, grouped_backward(): spread = spread.reshape(count, side, side, chans)  12.2 us
    all_to_all x1, starting transfers between devices, per_device(): lax.all_to_all(tokens, 'ctx', split_axis=0, concat_axis=0, tiled=True)  11.2 us
  transfers between devices with their start and end apart: 7, of which 4 were waited for; matrix products, arithmetic and copies ran while one was open for 19% of the time, Pallas kernels for 0%

commit v1 on v0

--- a/solution.py
+++ b/solution.py
@@ -152,9 +152,9 @@
     grad_hidden = jnp.stack([grad_even, grad_odd], axis=1).reshape(frames_dev, SIDE, SIDE, chans)
     grad_excite = jnp.sum(grad_hidden * active, axis=(1, 2))
     grad_inner = grad_excite * excite * (1.0 - excite)
-    grad_relaxed = lax.psum(
-        jnp.dot(grad_inner, squeeze_out.astype(jnp.float32).T, precision=highest), "tp"
-    )
+    x = jnp.dot(grad_inner, squeeze_out.astype(jnp.float32).T, precision=highest)
+    parts = lax.all_gather(x, "tp")
+    grad_relaxed = jnp.sum(parts, axis=0)
     grad_squeezed = grad_relaxed * silu_slope(squeezed)
     grad_pooled = jnp.dot(grad_squeezed, squeeze_in.astype(jnp.float32).T, precision=highest)
     grad_active = grad_hidden * excite[:, None, None, :] + grad_pooled[:, None, None, :] / cells

time: 349 us -> 357 us (1.023)
  blocking collectives: 34.3 us -> 42.3 us
    all_gather x0 -> x1, blocking collectives: none -> 24.7 us  [per_device(): parts = lax.all_gather(x, 'tp')]
    psum x1 -> x0, blocking collectives: 16.7 us -> none  [per_device(): lax.psum(jnp.dot(grad_inner, squeeze_out.astype(jnp.float32).T, precision...]
where the time goes in v1:
time: 357 us; the launch traced here: 356 us
  waiting for transfers between devices  187 us (52%)
  local copies, waits for them, and re-layouts  54.8 us (15%)
  blocking collectives  42.3 us (12%)
  starting transfers between devices  30.7 us (9%)
  matrix products  16 us (4%)
  between operations  15.9 us (4%)
  other arithmetic  9.61 us (3%)
    all_gather x1, waiting for transfers between devices, per_device(): lax.all_gather(sampler_kernel, 'ctx', axis=0, tiled=True)  81.3 us
    psum x1, waiting for transfers between devices, per_device(): grad_act = lax.psum(contract_last(back, full_readout), 'tp')  77.1 us
    all_gather x1, blocking collectives, per_device(): parts = lax.all_gather(x, 'tp')  24.7 us
    all_gather x1, waiting for transfers between devices, per_device(): lax.all_gather(readout_kernel, 'ctx', axis=0, tiled=True)  24.2 us
    psum x1, blocking collectives, per_device(): lax.psum(jnp.dot(pooled, squeeze_in.astype(jnp.float32), precision=highes...  17.6 us
    all_to_all x1, starting transfers between devices, per_device(): lax.all_to_all(token_cotangent, 'ctx', split_axis=0, concat_axis=0, tiled...  15.2 us
    reshape x9, local copies, waits for them, and re-layouts, grouped_backward(): spread = spread.reshape(count, side, side, chans)  12.2 us
    all_to_all x1, starting transfers between devices, per_device(): lax.all_to_all(tokens, 'ctx', split_axis=0, concat_axis=0, tiled=True)  11.2 us
  transfers between devices with their start and end apart: 7, of which 4 were waited for; matrix products, arithmetic and copies ran while one was open for 19% of the time, Pallas kernels for 0%

profile of v1, /device:TPU:6, one launch (start us, length us, event | category | flops | bytes accessed | tf_op | source)
XLA Modules:
  0.0 356.0 jit_solution(13159510728710075789)
XLA Ops:
  8.7 1.1 copy.230
  9.7 1.0 copy.240
  10.8 1.5 fusion.51
  12.4 2.3 pad_slice_fusion
  17.0 1.2 reshape.191
  18.2 0.8 copy.246
  19.0 2.0 reshape.192
  21.2 2.0 reshape.193
  27.1 17.6 %psum.21 = f32[2,288]{1,0:T(2,128)S(1)} all-reduce(f32[2,288]{1,0:T(2,128)S(1)} %fusion.53), channel_id=1, replica_groups=mesh['ctx'=64,'tp'=8] {'tp'}, use_global_device_ids=true, to_apply=%region_1.2 | all-reduce | flops 576 | bytes 4608 | tf_op jit(solution)/shard_map/psum | solution.py:98
  45.6 1.4 add_convert_fusion
  47.2 1.9 collective-permute-start
  51.1 15.2 %all-to-all-start.1 = ((bf16[64,2,512]{2,1,0:T(2,128)(2,1)}), bf16[64,2,512]{2,1,0:T(2,128)(2,1)S(1)}, u32[]{:S(2)}, u32[]{:S(2)}) async-start(bf16[64,2,512]{2,1,0:T(2,128)(2,1)} %reshape.229), calls=%async_computation.1 | async-start | bytes 262144 | tf_op jit(solution)/shard_map/all_to_all | solution.py:141
  71.6 0.9 reshape.196
  72.5 2.6 all-to-all-done.1
  75.3 24.2 %all-gather.8.cloned.1.call-done = bf16[64,18,1024]{2,1,0:T(8,128)(2,1)} async-done(((bf16[1,18,1024]{2,1,0:T(8,128)(2,1)}), bf16[64,18,1024]{2,1,0:T(8,128)(2,1)}) %all-gather.8.cloned.1.call-update) | async-done | bytes 2359312 | tf_op jit(solution)/shard_map/all_gather | solution.py:104
  99.5 2.9 reshape.213
  102.4 1.6 fusion.29
  104.0 81.3 %all-gather.6.cloned.1.call-done = bf16[1152,8,144]{2,1,0:T(8,128)(2,1)} async-done(((bf16[18,8,144]{2,1,0:T(8,128)(2,1)}), bf16[1152,8,144]{2,1,0:T(8,128)(2,1)}) %all-gather.6.cloned.1.call-update) | async-done | bytes 2654224 | tf_op jit(solution)/shard_map/all_gather | solution.py:103
  185.3 5.5 %copy.254 = bf16[1152,8,144]{0,2,1:T(8,128)(2,1)S(1)} copy(bf16[1152,8,144]{2,1,0:T(8,128)(2,1)} %all-gather.6.cloned.1.call-done) | data formatting | bytes 5308416 | tf_op jit(solution)/shard_map/all_gather | solution.py:103
  190.8 2.2 fusion.54
  193.1 77.1 %all-reduce.14.cloned.1.call-done = (f32[64,1152]{1,0:T(8,128)}, f32[64,1152]{1,0:T(8,128)}) async-done(((f32[64,1152]{1,0:T(8,128)}, f32[64,1152]{1,0:T(8,128)}), (f32[64,1152]{1,0:T(8,128)}, f32[64,1152]{1,0:T(8,128)})) %all-reduce.14.cloned.1.call-update) | async-done | bytes 589840 | tf_op jit(solution)/shard_map/psum | solution.py:144
  270.3 2.3 convolution_bitcast_fusion.14
  273.0 0.8 fusion.50
  273.8 2.1 collective-permute-start.1
  278.1 11.2 %all-to-all-start = ((bf16[64,2,512]{2,1,0:T(2,128)(2,1)}), bf16[64,2,512]{2,1,0:T(2,128)(2,1)S(1)}, u32[]{:S(2)}, u32[]{:S(2)}) async-start(bf16[64,2,512]{2,1,0:T(2,128)(2,1)} %reshape.231), calls=%async_computation | async-start | bytes 262144 | tf_op jit(solution)/shard_map/all_to_all | solution.py:139
  290.1 24.7 %all-gather.2 = f32[8,2,288]{2,1,0:T(2,128)S(1)} all-gather(f32[1,2,288]{2,1,0:T(2,128)S(1)} %convolution_bitcast_fusion.15), channel_id=2, replica_groups=mesh['ctx'=64,'tp'=8] {'tp'}, dimensions={0}, use_global_device_ids=true | all-gather | bytes 20736 | tf_op jit(solution)/shard_map/all_gather | solution.py:156
  316.1 1.1 convolution_bitcast_fusion.7
  317.2 1.1 convolution_bitcast_fusion.6
  318.3 1.1 convolution_bitcast_fusion.5
  319.4 1.1 convolution_bitcast_fusion.4
  320.6 1.1 convolution_bitcast_fusion.3
  322.8 1.3 reshape.201
  324.2 1.5 copy.264
  325.7 1.4 reshape.202
  327.0 1.5 copy.265
  328.5 1.4 reshape.203
  329.9 1.5 copy.266
  331.4 1.4 reshape.204
  332.8 1.5 copy.267
  334.3 1.4 reshape.205
  335.7 1.5 copy.268
  337.2 1.3 reshape.206
  338.9 1.4 reshape.207
  340.7 1.4 reshape.208
  342.5 1.4 reshape.209
  343.9 1.5 pad_add_fusion
  345.4 2.4 fusion.15
  347.8 0.8 copy.272
  (157 shorter events, 22.5 us)
Async XLA Ops:
  7.2 38.1 %copy-start = (bf16[288,144]{0,1:T(8,128)(2,1)S(1)}, bf16[288,144]{0,1:T(8,128)(2,1)}, u32[]{:S(2)}) copy-start(bf16[288,144]{0,1:T(8,128)(2,1)} %param.12) | copy-start | bytes 248836
  7.2 92.3 %all-gather.8.cloned.1.call-start = ((), (), s32[]{:S(2)}) async-start(), calls=%async_computation.3 | async-start | bytes 3194880 | tf_op jit(solution)/shard_map/all_gather | solution.py:104
  7.9 177.4 %all-gather.6.cloned.1.call-start = ((), (), s32[]{:S(2)}) async-start(), calls=%async_computation.2 | async-start | bytes 4792320 | tf_op jit(solution)/shard_map/all_gather | solution.py:103
  15.1 8.3 %copy-start.9 = (bf16[1,144,48]{2,1,0:T(8,128)(2,1)}, bf16[1,144,48]{2,1,0:T(8,128)(2,1)S(1)}, u32[]{:S(2)}) copy-start(bf16[1,144,48]{2,1,0:T(8,128)(2,1)S(1)} %copy.233) | copy-start | bytes 41476
  15.5 8.2 %copy-start.11 = (bf16[1,144,48]{2,1,0:T(8,128)(2,1)}, bf16[1,144,48]{2,1,0:T(8,128)(2,1)S(1)}, u32[]{:S(2)}) copy-start(bf16[1,144,48]{2,1,0:T(8,128)(2,1)S(1)} %copy.235) | copy-start | bytes 41476
  15.8 8.0 %copy-start.13 = (bf16[1,144,48]{2,1,0:T(8,128)(2,1)}, bf16[1,144,48]{2,1,0:T(8,128)(2,1)S(1)}, u32[]{:S(2)}) copy-start(bf16[1,144,48]{2,1,0:T(8,128)(2,1)S(1)} %copy.237) | copy-start | bytes 41476
  16.2 7.9 %copy-start.15 = (bf16[1,144,48]{2,1,0:T(8,128)(2,1)}, bf16[1,144,48]{2,1,0:T(8,128)(2,1)S(1)}, u32[]{:S(2)}) copy-start(bf16[1,144,48]{2,1,0:T(8,128)(2,1)S(1)} %copy.239) | copy-start | bytes 41476
  16.6 7.8 %copy-start.17 = (bf16[1,144,48]{2,1,0:T(8,128)(2,1)}, bf16[1,144,48]{2,1,0:T(8,128)(2,1)S(1)}, u32[]{:S(2)}) copy-start(bf16[1,144,48]{2,1,0:T(8,128)(2,1)S(1)} %copy.242) | copy-start | bytes 41476
  16.9 7.7 %copy-start.19 = (bf16[1,144,48]{2,1,0:T(8,128)(2,1)}, bf16[1,144,48]{2,1,0:T(8,128)(2,1)S(1)}, u32[]{:S(2)}) copy-start(bf16[1,144,48]{2,1,0:T(8,128)(2,1)S(1)} %copy.244) | copy-start | bytes 41476
  19.0 5.9 %copy-start.21 = (bf16[1,144,48]{2,1,0:T(8,128)(2,1)}, bf16[1,144,48]{2,1,0:T(8,128)(2,1)S(1)}, u32[]{:S(2)}) copy-start(bf16[1,144,48]{2,1,0:T(8,128)(2,1)S(1)} %copy.246) | copy-start | bytes 41476
  21.2 4.2 %copy-start.23 = (bf16[1,144,48]{2,1,0:T(8,128)(2,1)}, bf16[1,144,48]{2,1,0:T(8,128)(2,1)S(1)}, u32[]{:S(2)}) copy-start(bf16[1,144,48]{2,1,0:T(8,128)(2,1)S(1)} %copy.248) | copy-start | bytes 41476
  24.1 1.0 copy-start.7
  24.4 1.0 copy-start.8
  25.4 1.5 copy-start.26
  25.8 23.9 %copy-start.25 = (bf16[64,1024]{1,0:T(8,128)(2,1)S(1)}, bf16[64,1024]{1,0:T(8,128)(2,1)}, u32[]{:S(2)}) copy-start(bf16[64,1024]{1,0:T(8,128)(2,1)} %param.17) | copy-start | bytes 393220
  26.3 40.2 %copy-start.33 = (s32[128]{0:T(128)S(1)}, s32[128]{0:T(128)}, u32[]{:S(2)}) copy-start(s32[128]{0:T(128)} %param.15) | copy-start | bytes 1540
  26.3 43.2 %copy-start.34 = (s32[16]{0:T(128)S(1)}, s32[16]{0:T(128)}, u32[]{:S(2)}) copy-start(s32[16]{0:T(128)} %param.16) | copy-start | bytes 196
  44.7 0.6 copy-start.28
  47.2 23.6 %collective-permute-start = (bf16[14,14,144]{2,1,0:T(8,128)(2,1)S(1)}, bf16[14,14,144]{2,1,0:T(8,128)(2,1)S(1)}, u32[]{:S(2)}, u32[]{:S(2)}) collective-permute-start(bf16[14,14,144]{2,1,0:T(8,128)(2,1)S(1)} %bitcast.241), channel_id=1, source_target_pairs={{0,8},{8,16},{16,24},{24,32},{32,40},{40,48},{48,56},{56,64},{64,7... | collective-permute-start | bytes 169352 | tf_op jit(solution)/shard_map/ppermute | solution.py:13
  51.1 24.1 %all-to-all-start.1 = ((bf16[64,2,512]{2,1,0:T(2,128)(2,1)}), bf16[64,2,512]{2,1,0:T(2,128)(2,1)S(1)}, u32[]{:S(2)}, u32[]{:S(2)}) async-start(bf16[64,2,512]{2,1,0:T(2,128)(2,1)} %reshape.229), calls=%async_computation.1 | async-start | bytes 262144 | tf_op jit(solution)/shard_map/all_to_all | solution.py:141
  66.3 204.0 %all-reduce.14.cloned.1.call-start = ((), (), s32[]{:S(2)}) async-start(), calls=%async_computation.4 | async-start | bytes 1179648 | tf_op jit(solution)/shard_map/psum | solution.py:144
  70.8 31.6 %copy-start.30 = (bf16[64]{0:T(256)(128)(2,1)}, bf16[64]{0:T(256)(128)(2,1)S(1)}, u32[]{:S(2)}) copy-start(bf16[64]{0:T(256)(128)(2,1)S(1)} %compare_convert_fusion) | copy-start | bytes 388
  102.4 1.6 copy-start.1
  270.3 5.6 %copy-start.2 = (bf16[1152,1024]{1,0:T(8,128)(2,1)S(1)}, bf16[1152,1024]{1,0:T(8,128)(2,1)}, u32[]{:S(2)}) copy-start(bf16[1152,1024]{1,0:T(8,128)(2,1)} %copy-done.1) | copy-start | bytes 7077892
  270.3 5.6 %copy-start.31 = (bf16[64]{0:T(256)(128)(2,1)S(1)}, bf16[64]{0:T(256)(128)(2,1)}, u32[]{:S(2)}) copy-start(bf16[64]{0:T(256)(128)(2,1)} %copy-done.30) | copy-start | bytes 388
  270.3 5.6 %copy-start.32 = (f32[64,1152]{1,0:T(8,128)S(1)}, f32[64,1152]{1,0:T(8,128)}, u32[]{:S(2)}) copy-start(f32[64,1152]{1,0:T(8,128)} %get-tuple-element.15) | copy-start | bytes 884740
  273.8 15.7 %copy-start.3 = (f32[2,14,14,144]{3,0,2,1:T(2,128)S(1)}, f32[2,14,14,144]{3,0,2,1:T(2,128)}, u32[]{:S(2)}) copy-start(f32[2,14,14,144]{3,0,2,1:T(2,128)} %get-tuple-element.17) | copy-start | bytes 677380
  273.8 41.1 %copy-start.27 = (bf16[144,288]{1,0:T(8,128)(2,1)S(1)}, bf16[144,288]{1,0:T(8,128)(2,1)}, u32[]{:S(2)}) copy-start(bf16[144,288]{1,0:T(8,128)(2,1)} %param.11) | copy-start | bytes 248836
  273.8 41.1 %copy-start.29 = (f32[2,288]{1,0:T(2,128)S(1)}, f32[2,288]{1,0:T(2,128)}, u32[]{:S(2)}) copy-start(f32[2,288]{1,0:T(2,128)} %copy-done.28) | copy-start | bytes 6916
  273.8 15.5 %collective-permute-start.1 = (bf16[14,14,144]{2,1,0:T(8,128)(2,1)S(1)}, bf16[14,14,144]{2,1,0:T(8,128)(2,1)S(1)}, u32[]{:S(2)}, u32[]{:S(2)}) collective-permute-start(bf16[14,14,144]{2,1,0:T(8,128)(2,1)S(1)} %fusion.31), channel_id=1, source_target_pairs={{8,0},{16,8},{24,16},{32,24},{40,32},{48,40},{56,48},{64,56},{72,6... | collective-permute-start | bytes 169352 | tf_op jit(solution)/shard_map/ppermute | solution.py:13
  278.1 70.5 %all-to-all-start = ((bf16[64,2,512]{2,1,0:T(2,128)(2,1)}), bf16[64,2,512]{2,1,0:T(2,128)(2,1)S(1)}, u32[]{:S(2)}, u32[]{:S(2)}) async-start(bf16[64,2,512]{2,1,0:T(2,128)(2,1)} %reshape.231), calls=%async_computation | async-start | bytes 262144 | tf_op jit(solution)/shard_map/all_to_all | solution.py:139
  289.4 26.7 %copy-start.10 = (bf16[1,144,48]{2,1,0:T(8,128)(2,1)S(1)}, bf16[1,144,48]{2,1,0:T(8,128)(2,1)}, u32[]{:S(2)}) copy-start(bf16[1,144,48]{2,1,0:T(8,128)(2,1)} %copy-done.9) | copy-start | bytes 41476
  290.1 27.1 %copy-start.12 = (bf16[1,144,48]{2,1,0:T(8,128)(2,1)S(1)}, bf16[1,144,48]{2,1,0:T(8,128)(2,1)}, u32[]{:S(2)}) copy-start(bf16[1,144,48]{2,1,0:T(8,128)(2,1)} %copy-done.11) | copy-start | bytes 41476
  315.5 2.9 copy-start.14
  315.5 3.9 %copy-start.16 = (bf16[1,144,48]{2,1,0:T(8,128)(2,1)S(1)}, bf16[1,144,48]{2,1,0:T(8,128)(2,1)}, u32[]{:S(2)}) copy-start(bf16[1,144,48]{2,1,0:T(8,128)(2,1)} %copy-done.15) | copy-start | bytes 41476
  315.8 4.7 %copy-start.18 = (bf16[1,144,48]{2,1,0:T(8,128)(2,1)S(1)}, bf16[1,144,48]{2,1,0:T(8,128)(2,1)}, u32[]{:S(2)}) copy-start(bf16[1,144,48]{2,1,0:T(8,128)(2,1)} %copy-done.17) | copy-start | bytes 41476
  316.1 5.5 %copy-start.20 = (bf16[1,144,48]{2,1,0:T(8,128)(2,1)S(1)}, bf16[1,144,48]{2,1,0:T(8,128)(2,1)}, u32[]{:S(2)}) copy-start(bf16[1,144,48]{2,1,0:T(8,128)(2,1)} %copy-done.19) | copy-start | bytes 41476
  317.2 4.7 %copy-start.22 = (bf16[1,144,48]{2,1,0:T(8,128)(2,1)S(1)}, bf16[1,144,48]{2,1,0:T(8,128)(2,1)}, u32[]{:S(2)}) copy-start(bf16[1,144,48]{2,1,0:T(8,128)(2,1)} %copy-done.21) | copy-start | bytes 41476
  318.3 3.8 %copy-start.24 = (bf16[1,144,48]{2,1,0:T(8,128)(2,1)S(1)}, bf16[1,144,48]{2,1,0:T(8,128)(2,1)}, u32[]{:S(2)}) copy-start(bf16[1,144,48]{2,1,0:T(8,128)(2,1)} %copy-done.23) | copy-start | bytes 41476
  340.3 3.6 %copy-start.4 = (f32[2,14,14,144]{3,0,2,1:T(2,128)S(1)}, f32[2,14,14,144]{3,0,2,1:T(2,128)}, u32[]{:S(2)}) copy-start(f32[2,14,14,144]{3,0,2,1:T(2,128)} %reshape.201) | copy-start | bytes 677380
  342.1 3.3 copy-start.5
  342.5 2.9 copy-start.6
Sparse Core Ops, SparseCore 0:
  11.3 88.0 all-gather.7
  102.8 82.4 all-gather.5
  193.2 77.0 all-reduce.13
